TPU v7x, 256 devices: a whole 4x4x8 slice. The times are simulated.
256 devices in a mesh: tok: 16 (over x, y_hi, core), col: 8 (over z), grp: 2 (over y_lo).
Axes of the slice: x: 4, y: 4 (y_hi: 2, y_lo: 2; y = y_hi * 2 + y_lo), z: 8, core: 2. Of those that a mesh axis runs over, the one named last changes fastest.
Arguments:
- calibration: bfloat16 [24576, 4096], P(('tok', 'grp'), 'col'), may hold values from -1.1 to 1.1
- weight: float32 [4096, 4096], P(('tok', 'grp'), 'col'), may hold values from -6 to 6
- tile_mask: int32 [32, 32], P(('tok', 'grp'), 'col'), may hold values 0 or 1
- token_ids: int32 [2048], P(('tok', 'grp')), may hold values from 0 to 767
Outputs:
- new_weight: bfloat16 [4096, 4096], P(('tok', 'grp'), 'col')
- outputs: bfloat16 [2048, 4096], P('col', ('tok', 'grp'))
All inputs are finite; a program needn't handle non-finite values. No bound on the sum of `tile_mask` on one device may be relied on, other than what follows from the above.
Results may differ from a plain program's by a relative error of at most 0.0019.
The roundings to bfloat16 on the way count: a program that leaves them out, or rounds other values in their place, can miss the bound.
Values may be sent and summed in bfloat16 or wider, within the bound.
No kernel may reach another device: no remote copies, remote signals or barrier semaphores. Data moves between devices by JAX's collectives and lax.ppermute only.
A program may use at most 64 MiB of HBM per device.

v0:
```python
import jax
import jax.numpy as jnp
from jax import lax
from jax.sharding import PartitionSpec as P

TILE = 128
ITERS = 3
DAMPING = 0.1


def expand_tiles(tile_flags):
    tile_rows, tile_cols = tile_flags.shape
    expanded = jnp.broadcast_to(
        tile_flags.astype(jnp.float32)[:, None, :, None], (tile_rows, TILE, tile_cols, TILE)
    )
    return expanded.reshape(tile_rows * TILE, tile_cols * TILE)


def per_device(calibration, weight, tile_mask, token_ids):
    col_width = calibration.shape[1]
    col_count = lax.axis_size("col")
    width = col_width * col_count
    col_place = lax.axis_index("col")
    squares = jnp.sum(jnp.square(calibration.astype(jnp.float32)))
    trace_total = lax.psum(squares, ("tok", "col", "grp"))
    partial_gram = lax.dot_general(
        calibration,
        lax.all_gather(calibration, "col", axis=1, tiled=True),
        (((0,), (0,)), ((), ())),
        preferred_element_type=jnp.float32,
    )
    gram_slice = lax.psum_scatter(partial_gram, ("tok", "grp"), scatter_dimension=1, tiled=True)
    gram_rows = lax.all_gather(gram_slice, ("tok", "grp"), axis=1, tiled=True)
    trace_scale = trace_total / width
    row_ids = col_place * col_width + lax.broadcasted_iota(jnp.int32, gram_rows.shape, 0)
    col_ids = lax.broadcasted_iota(jnp.int32, gram_rows.shape, 1)
    stationary = gram_rows / trace_scale + jnp.where(row_ids == col_ids, DAMPING, 0.0)

    def apply_gram(operand):
        return lax.dot_general(
            lax.all_gather(operand, "col", axis=1, tiled=True),
            stationary,
            (((1,), (1,)), ((), ())),
            precision=lax.Precision.HIGHEST,
            preferred_element_type=jnp.float32,
        )

    keep_mask = expand_tiles(tile_mask)
    current = weight * keep_mask
    residual = apply_gram(current - weight)
    for iteration in range(ITERS):
        gradient = residual * keep_mask
        image_rows = apply_gram(gradient)
        sums_pair = lax.psum(
            (jnp.sum(gradient * gradient), jnp.sum(gradient * image_rows)), ("tok", "col", "grp")
        )
        length = sums_pair[0] / sums_pair[1]
        current = current - length * gradient
        if iteration + 1 < ITERS:
            residual = residual - length * image_rows
    new_weight = current.astype(jnp.bfloat16)
    chosen = jnp.take(calibration, token_ids, axis=0)
    all_chosen = lax.all_gather(chosen, ("tok", "grp"), axis=0, tiled=True)
    outputs = lax.psum_scatter(
        lax.dot_general(
            all_chosen, new_weight, (((1,), (1,)), ((), ())), preferred_element_type=jnp.float32
        ),
        "col",
        scatter_dimension=0,
        tiled=True,
    )
    return (new_weight, outputs.astype(jnp.bfloat16))


def solution(mesh):
    placed = (
        P(("tok", "grp"), "col"),
        P(("tok", "grp"), "col"),
        P(("tok", "grp"), "col"),
        P(("tok", "grp")),
    )
    return jax.shard_map(
        per_device,
        mesh=mesh,
        in_specs=placed,
        out_specs=(P(("tok", "grp"), "col"), P("col", ("tok", "grp"))),
        check_vma=False,
    )
```

profile of v0, /device:TPU:2, one launch (start us, length us, event | category | flops | bytes accessed | tf_op | source)
XLA Modules:
  0.0 833.4 jit_solution(12873526358352657317)
XLA Ops:
  7.2 0.0 all-gather.10.cloned.1.call-start
  7.2 0.7 all-gather.10.cloned.1.call-update
  7.9 0.0 reduce-scatter.3.cloned.1.call-start
  7.9 79.3 %all-gather.10.cloned.1.call-done = bf16[768,4096]{1,0:T(8,128)(2,1)} async-done(((bf16[768,512]{1,0:T(8,128)(2,1)}), bf16[768,4096]{1,0:T(8,128)(2,1)}) %all-gather.10.cloned.1.call-update) | async-done | bytes 6291472 | tf_op jit(solution)/shard_map/all_gather | solution.py:28
  87.3 9.7 %fusion.4 = f32[512,4096]{1,0:T(8,128)} fusion(bf16[768,512]{1,0:T(8,128)(2,1)} %param.4, bf16[768,4096]{1,0:T(8,128)(2,1)} %all-gather.10.cloned.1.call-done), kind=kOutput, calls=%fused_computation.27 | convolution fusion | flops 3221225472 | bytes 15466496 | tf_op jit(solution)/shard_map/dot_general | solution.py:26
  97.0 0.0 copy-start.6
  97.0 0.0 copy-start.4
  97.0 0.0 copy-start
  97.0 0.0 reduce-scatter.3.cloned.1.call-update
  97.0 0.0 all-gather.12.cloned.1.call-start
  97.1 143.3 %reduce-scatter.3.cloned.1.call-done = f32[512,128]{1,0:T(8,128)} async-done(((f32[512,4096]{1,0:T(8,128)}), f32[512,128]{1,0:T(8,128)}) %reduce-scatter.3.cloned.1.call-update) | async-done | bytes 262160 | tf_op jit(solution)/shard_map/reduce_scatter | solution.py:32
  240.4 0.0 all-gather.12.cloned.1.call-update
  240.4 0.0 all-gather.8.cloned.1.call-start
  240.5 0.0 copy-done.6
  240.5 0.1 broadcast_bitcast_fusion
  240.6 0.0 copy-done.4
  240.6 0.7 multiply_subtract_fusion.1
  241.3 0.0 all-gather.8.cloned.1.call-update
  241.3 0.0 all-gather.14.cloned.1.call-start
  241.4 0.0 copy-done
  241.4 1.0 multiply_reduce_fusion
  242.4 77.8 %psum.49 = f32[]{:T(128)} all-reduce(f32[]{:T(128)} %multiply_reduce_fusion), channel_id=1, replica_groups=mesh['tok'=16,'col'=8,'grp'=2] {'tok','col','grp'}, use_global_device_ids=true, to_apply=%region_2.0 | all-reduce | flops 1 | bytes 8 | tf_op jit(solution)/shard_map/psum | solution.py:25
  320.8 22.7 %all-gather.12.cloned.1.call-done = f32[512,4096]{1,0:T(8,128)} async-done(((f32[512,128]{1,0:T(8,128)}), f32[512,4096]{1,0:T(8,128)}) %all-gather.12.cloned.1.call-update) | async-done | bytes 8388624 | tf_op jit(solution)/shard_map/all_gather | solution.py:33
  343.5 6.3 select_add_fusion
  349.8 36.7 %all-gather.8.cloned.1.call-done = f32[128,4096]{1,0:T(8,128)} async-done(((f32[128,512]{1,0:T(8,128)}), f32[128,4096]{1,0:T(8,128)}) %all-gather.8.cloned.1.call-update) | async-done | bytes 2097168 | tf_op jit(solution)/shard_map/all_gather | solution.py:41
  386.5 13.5 %broadcast_multiply_fusion.1 = (f32[128,512]{1,0:T(8,128)}, f32[128,512]{1,0:T(8,128)S(1)}) fusion(f32[512]{0:T(512)S(1)} %broadcast_bitcast_fusion, f32[128,4096]{1,0:T(8,128)} %all-gather.8.cloned.1.call-done, f32[512,4096]{1,0:T(8,128)} %select_add_fusion), kind=kOutput, calls=%fused_computation.19 | convolution fusion | flops 3221291008 | bytes 11012096 | tf_op jit(solution)/shard_map/dot_general | solution.py:40
  400.0 0.0 all-gather.14.cloned.1.call-update
  400.0 0.6 all-gather.16.cloned.1.call-start
  400.6 39.3 %all-gather.14.cloned.1.call-done = f32[128,4096]{1,0:T(8,128)} async-done(((f32[128,512]{1,0:T(8,128)}), f32[128,4096]{1,0:T(8,128)}) %all-gather.14.cloned.1.call-update) | async-done | bytes 2097168 | tf_op jit(solution)/shard_map/all_gather | solution.py:41
  439.8 13.4 %multiply_reduce_fusion.4 = (f32[]{:T(128)}, f32[]{:T(128)}, f32[128,512]{1,0:T(8,128)S(1)}) fusion(f32[128,512]{1,0:T(8,128)} %get-tuple-element.14, f32[128,4096]{1,0:T(8,128)} %all-gather.14.cloned.1.call-done, f32[512,4096]{1,0:T(8,128)} %select_add_fusion), kind=kOutput, calls=%fused_computation.16 | convolution fusion | flops 3221487616 | bytes 11010056 | tf_op jit(solution)/shard_map/dot_general | solution.py:40
  453.2 74.2 %all-reduce.2 = (f32[]{:T(128)}, f32[]{:T(128)}) all-reduce(f32[]{:T(128)} %get-tuple-element.5, f32[]{:T(128)} %get-tuple-element.4), channel_id=1, replica_groups=mesh['tok'=16,'col'=8,'grp'=2] {'tok','col','grp'}, use_global_device_ids=true, to_apply=%region_4.5 | all-reduce | flops 2 | bytes 16 | tf_op jit(solution)/shard_map/psum | solution.py:54
  528.7 0.8 broadcast_multiply_fusion
  529.5 0.0 copy-start.7
  529.5 0.0 all-gather.16.cloned.1.call-update
  529.5 0.2 all-gather.18.cloned.1.call-start
  529.8 37.6 %all-gather.16.cloned.1.call-done = f32[128,4096]{1,0:T(8,128)} async-done(((f32[128,512]{1,0:T(8,128)}), f32[128,4096]{1,0:T(8,128)}) %all-gather.16.cloned.1.call-update) | async-done | bytes 2097168 | tf_op jit(solution)/shard_map/all_gather | solution.py:41
  567.4 13.4 %multiply_reduce_fusion.2 = (f32[]{:T(128)}, f32[]{:T(128)}, f32[128,512]{1,0:T(8,128)S(1)}) fusion(f32[128,512]{1,0:T(8,128)} %broadcast_multiply_fusion, f32[128,4096]{1,0:T(8,128)} %all-gather.16.cloned.1.call-done, f32[512,4096]{1,0:T(8,128)} %select_add_fusion), kind=kOutput, calls=%fused_computation.13 | convolution fusion | flops 3221487616 | bytes 11010056 | tf_op jit(solution)/shard_map/dot_general | solution.py:40
  580.8 74.2 %all-reduce.1 = (f32[]{:T(128)}, f32[]{:T(128)}) all-reduce(f32[]{:T(128)} %get-tuple-element.3, f32[]{:T(128)} %get-tuple-element.2), channel_id=1, replica_groups=mesh['tok'=16,'col'=8,'grp'=2] {'tok','col','grp'}, use_global_device_ids=true, to_apply=%region_8.9 | all-reduce | flops 2 | bytes 16 | tf_op jit(solution)/shard_map/psum | solution.py:54
  656.3 0.0 copy-start.1
  656.3 0.0 copy-start.3
  656.3 1.4 multiply_reduce_fusion.1
  657.7 0.0 copy-start.2
  657.7 0.0 all-gather.18.cloned.1.call-update
  657.8 0.0 all-gather.20.cloned.1.call-start
  657.8 0.0 copy-done.7
  657.9 0.7 gather_fusion
  658.6 0.7 broadcast_select_fusion
  659.3 0.0 all-gather.20.cloned.1.call-update
  659.3 0.3 reduce-scatter.5.cloned.1.call-start
  659.6 36.1 %all-gather.18.cloned.1.call-done = f32[128,4096]{1,0:T(8,128)} async-done(((f32[128,512]{1,0:T(8,128)}), f32[128,4096]{1,0:T(8,128)}) %all-gather.18.cloned.1.call-update) | async-done | bytes 2097168 | tf_op jit(solution)/shard_map/all_gather | solution.py:41
  695.7 13.4 %fusion = f32[]{:T(128)} fusion(f32[128,512]{1,0:T(8,128)} %get-tuple-element.13, f32[128,4096]{1,0:T(8,128)} %all-gather.18.cloned.1.call-done, f32[512,4096]{1,0:T(8,128)} %select_add_fusion), kind=kOutput, calls=%fused_computation.5 | convolution fusion | flops 3221356544 | bytes 10747908 | tf_op jit(solution)/shard_map/dot_general | solution.py:40
  709.0 74.2 %all-reduce = (f32[]{:T(128)}, f32[]{:T(128)}) all-reduce(f32[]{:T(128)} %get-tuple-element.12, f32[]{:T(128)} %fusion), channel_id=1, replica_groups=mesh['tok'=16,'col'=8,'grp'=2] {'tok','col','grp'}, use_global_device_ids=true, to_apply=%region_12.13 | all-reduce | flops 2 | bytes 16 | tf_op jit(solution)/shard_map/psum | solution.py:54
  784.6 0.0 copy-done.1
  784.6 0.0 copy-done.3
  784.6 0.0 copy-done.2
  784.6 0.1 fusion.3
  784.8 0.0 copy-start.5
  784.8 0.0 all-gather.20.cloned.1.call-done
  784.8 3.3 fusion.5
  788.1 0.0 reduce-scatter.5.cloned.1.call-update
  788.1 37.0 %reduce-scatter.5.cloned.1.call-done = f32[256,128]{1,0:T(8,128)} async-done(((f32[2048,128]{1,0:T(8,128)}), f32[256,128]{1,0:T(8,128)}) %reduce-scatter.5.cloned.1.call-update) | async-done | bytes 131088 | tf_op jit(solution)/shard_map/reduce_scatter | solution.py:64
  825.1 1.5 convert_element_type.15
  826.6 0.0 copy-done.5
  (5 shorter events, 0.0 us)
Async XLA Ops:
  7.2 80.1 %all-gather.10.cloned.1.call-start = ((), (), s32[]{:S(2)}) async-start(), calls=%async_computation.3 | async-start | bytes 7077888 | tf_op jit(solution)/shard_map/all_gather | solution.py:28
  7.9 232.5 %reduce-scatter.3.cloned.1.call-start = ((), (), s32[]{:S(2)}) async-start(), calls=%async_computation.4 | async-start | bytes 8650752 | tf_op jit(solution)/shard_map/reduce_scatter | solution.py:32
  97.0 143.5 %copy-start.6 = (s32[1,4]{1,0:T(1,128)S(1)}, s32[1,4]{1,0:T(1,128)}, u32[]{:S(2)}) copy-start(s32[1,4]{1,0:T(1,128)} %param.6) | copy-start | bytes 52
  97.0 143.6 %copy-start.4 = (f32[128,512]{1,0:T(8,128)S(1)}, f32[128,512]{1,0:T(8,128)}, u32[]{:S(2)}) copy-start(f32[128,512]{1,0:T(8,128)} %param.5) | copy-start | bytes 786436
  97.0 144.4 %copy-start = (bf16[768,512]{1,0:T(8,128)(2,1)S(1)}, bf16[768,512]{1,0:T(8,128)(2,1)}, u32[]{:S(2)}) copy-start(bf16[768,512]{1,0:T(8,128)(2,1)} %param.4) | copy-start | bytes 2359300
  97.0 246.5 %all-gather.12.cloned.1.call-start = ((), (), s32[]{:S(2)}) async-start(), calls=%async_computation.5 | async-start | bytes 8650752 | tf_op jit(solution)/shard_map/all_gather | solution.py:33
  240.4 146.1 %all-gather.8.cloned.1.call-start = ((), (), s32[]{:S(2)}) async-start(), calls=%async_computation.2 | async-start | bytes 2359296 | tf_op jit(solution)/shard_map/all_gather | solution.py:41
  241.3 198.5 %all-gather.14.cloned.1.call-start = ((), (), s32[]{:S(2)}) async-start(), calls=%async_computation.6 | async-start | bytes 2359296 | tf_op jit(solution)/shard_map/all_gather | solution.py:41
  400.0 167.4 %all-gather.16.cloned.1.call-start = ((), (), s32[]{:S(2)}) async-start(), calls=%async_computation.7 | async-start | bytes 2359296 | tf_op jit(solution)/shard_map/all_gather | solution.py:41
  529.5 128.3 %copy-start.7 = (s32[64]{0:T(128)S(1)}, s32[64]{0:T(128)}, u32[]{:S(2)}) copy-start(s32[64]{0:T(128)} %param.7) | copy-start | bytes 772
  529.5 166.1 %all-gather.18.cloned.1.call-start = ((), (), s32[]{:S(2)}) async-start(), calls=%async_computation.8 | async-start | bytes 2359296 | tf_op jit(solution)/shard_map/all_gather | solution.py:41
  656.3 128.3 %copy-start.1 = (f32[128,512]{1,0:T(8,128)S(1)}, f32[128,512]{1,0:T(8,128)}, u32[]{:S(2)}) copy-start(f32[128,512]{1,0:T(8,128)} %get-tuple-element.14) | copy-start | bytes 786436
  656.3 128.3 %copy-start.3 = (f32[128,512]{1,0:T(8,128)S(1)}, f32[128,512]{1,0:T(8,128)}, u32[]{:S(2)}) copy-start(f32[128,512]{1,0:T(8,128)} %broadcast_multiply_fusion) | copy-start | bytes 786436
  657.7 126.9 %copy-start.2 = (f32[128,512]{1,0:T(8,128)S(1)}, f32[128,512]{1,0:T(8,128)}, u32[]{:S(2)}) copy-start(f32[128,512]{1,0:T(8,128)} %get-tuple-element.13) | copy-start | bytes 786436
  657.8 127.0 %all-gather.20.cloned.1.call-start = ((), (), s32[]{:S(2)}) async-start(), calls=%async_computation.9 | async-start | bytes 2162688 | tf_op jit(solution)/shard_map/all_gather | solution.py:63
  659.3 165.8 %reduce-scatter.5.cloned.1.call-start = ((), (), s32[]{:S(2)}) async-start(), calls=%async_computation.10 | async-start | bytes 1179648 | tf_op jit(solution)/shard_map/reduce_scatter | solution.py:64
  784.8 41.9 %copy-start.5 = (bf16[128,512]{1,0:T(8,128)(2,1)}, bf16[128,512]{1,0:T(8,128)(2,1)S(1)}, u32[]{:S(2)}) copy-start(bf16[128,512]{1,0:T(8,128)(2,1)S(1)} %fusion.3) | copy-start | bytes 393220
Sparse Core Ops, SparseCore 0:
  9.8 77.4 all-gather.9
  97.2 143.1 reduce-scatter.2
  242.1 101.3 all-gather.11
  345.2 41.3 all-gather.7
  400.1 39.6 all-gather.13
  529.7 37.7 all-gather.15
  657.9 37.7 all-gather.17
  698.0 84.5 all-gather.19
  788.3 36.8 reduce-scatter.4
where the time goes:
time: 838 us; the launch traced here: 833 us
  waiting for transfers between devices  433 us (52%)
  blocking collectives  300 us (36%)
  matrix products  66.6 us (8%)
  between operations  18.9 us (2%)
  other arithmetic  12.6 us (2%)
    psum x3, blocking collectives, per_device(): lax.psum((jnp.sum(gradient * gradient), jnp.sum(gradient * image_rows)),...  223 us
    all_gather x4, waiting for transfers between devices, apply_gram(): lax.all_gather(operand, 'col', axis=1, tiled=True)  150 us
    reduce_scatter x1, waiting for transfers between devices, per_device(): lax.psum_scatter(partial_gram, ('tok', 'grp'), scatter_dimension=1, tiled...  143 us
    all_gather x1, waiting for transfers between devices, per_device(): lax.all_gather(calibration, 'col', axis=1, tiled=True)  79.3 us
    psum x1, blocking collectives, per_device(): trace_total = lax.psum(squares, ('tok', 'col', 'grp'))  77.8 us
    dot_general x4, matrix products, apply_gram(): lax.dot_general(lax.all_gather(operand, 'col', axis=1, tiled=True), stati...  53.5 us
    reduce_scatter x1, waiting for transfers between devices, per_device(): lax.psum_scatter(lax.dot_general(all_chosen, new_weight, (((1,), (1,)), (...  37 us
    all_gather x1, waiting for transfers between devices, per_device(): gram_rows = lax.all_gather(gram_slice, ('tok', 'grp'), axis=1, tiled=True)  22.7 us
  transfers between devices with their start and end apart: 9, of which 8 were waited for; matrix products, arithmetic and copies ran while one was open for 3% of the time, Pallas kernels for 0%

commit v1 on v0

--- a/solution.py
+++ b/solution.py
@@ -6,6 +6,13 @@
 TILE = 128
 ITERS = 3
 DAMPING = 0.1
+
+
+def exchange_gather(x, axis, along):
+    size = lax.axis_size(axis)
+    blocks = jnp.stack([x for _ in range(size)])
+    blocks = lax.all_to_all(blocks, axis, split_axis=0, concat_axis=0)
+    return jnp.concatenate(blocks, axis=along)
 
 
 def expand_tiles(tile_flags):
@@ -25,7 +32,7 @@
     trace_total = lax.psum(squares, ("tok", "col", "grp"))
     partial_gram = lax.dot_general(
         calibration,
-        lax.all_gather(calibration, "col", axis=1, tiled=True),
+        exchange_gather(calibration, "col", 1),
         (((0,), (0,)), ((), ())),
         preferred_element_type=jnp.float32,
     )

time: 838 us -> 908 us (1.084)
  blocking collectives: 300 us -> 450 us
  waiting for transfers between devices: 433 us -> 351 us
    all_to_all x0 -> x1, blocking collectives: none -> 149 us  [exchange_gather(): blocks = lax.all_to_all(blocks, axis, split_axis=0, concat_axis=0)]
    all_gather x1 -> x0, waiting for transfers between devices: 79.3 us -> none  [per_device(): lax.all_gather(calibration, 'col', axis=1, tiled=True)]
  transfers between devices with their start and end apart: 9 -> 8, of which waited for: 8 -> 7; matrix products, arithmetic and copies ran while one was open for 3% -> 3% of each run, Pallas kernels for 0% -> 0%
where the time goes in v1:
time: 908 us; the launch traced here: 898 us
  blocking collectives  450 us (50%)
  waiting for transfers between devices  351 us (39%)
  matrix products  62.5 us (7%)
  between operations  19.1 us (2%)
  other arithmetic  12.6 us (1%)
    psum x3, blocking collectives, per_device(): lax.psum((jnp.sum(gradient * gradient), jnp.sum(gradient * image_rows)),...  223 us
    all_gather x4, waiting for transfers between devices, apply_gram(): lax.all_gather(operand, 'col', axis=1, tiled=True)  150 us
    all_to_all x1, blocking collectives, exchange_gather(): blocks = lax.all_to_all(blocks, axis, split_axis=0, concat_axis=0)  149 us
    reduce_scatter x1, waiting for transfers between devices, per_device(): lax.psum_scatter(partial_gram, ('tok', 'grp'), scatter_dimension=1, tiled...  141 us
    psum x1, blocking collectives, per_device(): trace_total = lax.psum(squares, ('tok', 'col', 'grp'))  77.4 us
    dot_general x4, matrix products, apply_gram(): lax.dot_general(lax.all_gather(operand, 'col', axis=1, tiled=True), stati...  53.5 us
    reduce_scatter x1, waiting for transfers between devices, per_device(): lax.psum_scatter(lax.dot_general(all_chosen, new_weight, (((1,), (1,)), (...  36.9 us
    all_gather x1, waiting for transfers between devices, per_device(): gram_rows = lax.all_gather(gram_slice, ('tok', 'grp'), axis=1, tiled=True)  22.9 us
  transfers between devices with their start and end apart: 8, of which 7 were waited for; matrix products, arithmetic and copies ran while one was open for 3% of the time, Pallas kernels for 0%

profile of v1, /device:TPU:2, one launch (start us, length us, event | category | flops | bytes accessed | tf_op | source)
XLA Modules:
  0.0 898.4 jit_solution(10332964519267958768)
XLA Ops:
  7.2 0.0 reduce-scatter.3.cloned.1.call-start
  7.2 1.4 copy.6
  8.6 0.4 stack.2
  9.0 0.0 copy-start
  9.0 149.5 %all_to_all.5 = bf16[8,768,512]{1,2,0:T(8,128)(2,1)S(1)} all-to-all(bf16[8,768,512]{1,2,0:T(8,128)(2,1)S(1)} %stack.2), channel_id=1, replica_groups=mesh['tok'=16,'col'=8,'grp'=2] {'col'}, dimensions={0} | all-to-all | bytes 12582912 | tf_op jit(solution)/shard_map/all_to_all | solution.py:14
  158.5 0.0 copy-done
  158.5 5.7 fusion.4
  164.2 0.0 copy-start.6
  164.2 0.0 copy-start.4
  164.2 0.0 reduce-scatter.3.cloned.1.call-update
  164.2 0.0 all-gather.9.cloned.1.call-start
  164.3 141.0 %reduce-scatter.3.cloned.1.call-done = f32[512,128]{1,0:T(8,128)} async-done(((f32[512,4096]{1,0:T(8,128)}), f32[512,128]{1,0:T(8,128)}) %reduce-scatter.3.cloned.1.call-update) | async-done | bytes 262160 | tf_op jit(solution)/shard_map/reduce_scatter | solution.py:39
  305.3 0.0 all-gather.9.cloned.1.call-update
  305.3 0.0 all-gather.7.cloned.1.call-start
  305.4 0.0 copy-done.6
  305.4 0.1 broadcast_bitcast_fusion
  305.5 0.0 copy-done.4
  305.5 0.7 multiply_subtract_fusion.1
  306.2 0.0 all-gather.7.cloned.1.call-update
  306.3 0.0 all-gather.11.cloned.1.call-start
  306.3 1.0 multiply_reduce_fusion
  307.3 77.4 %psum.49 = f32[]{:T(128)} all-reduce(f32[]{:T(128)} %multiply_reduce_fusion), channel_id=1, replica_groups=mesh['tok'=16,'col'=8,'grp'=2] {'tok','col','grp'}, use_global_device_ids=true, to_apply=%region_2.0 | all-reduce | flops 1 | bytes 8 | tf_op jit(solution)/shard_map/psum | solution.py:32
  385.3 22.9 %all-gather.9.cloned.1.call-done = f32[512,4096]{1,0:T(8,128)} async-done(((f32[512,128]{1,0:T(8,128)}), f32[512,4096]{1,0:T(8,128)}) %all-gather.9.cloned.1.call-update) | async-done | bytes 8388624 | tf_op jit(solution)/shard_map/all_gather | solution.py:40
  408.2 6.3 select_add_fusion
  414.5 36.8 %all-gather.7.cloned.1.call-done = f32[128,4096]{1,0:T(8,128)} async-done(((f32[128,512]{1,0:T(8,128)}), f32[128,4096]{1,0:T(8,128)}) %all-gather.7.cloned.1.call-update) | async-done | bytes 2097168 | tf_op jit(solution)/shard_map/all_gather | solution.py:48
  451.3 13.5 %broadcast_multiply_fusion.1 = (f32[128,512]{1,0:T(8,128)}, f32[128,512]{1,0:T(8,128)S(1)}) fusion(f32[512]{0:T(512)S(1)} %broadcast_bitcast_fusion, f32[128,4096]{1,0:T(8,128)} %all-gather.7.cloned.1.call-done, f32[512,4096]{1,0:T(8,128)} %select_add_fusion), kind=kOutput, calls=%fused_computation.19 | convolution fusion | flops 3221291008 | bytes 11012096 | tf_op jit(solution)/shard_map/dot_general | solution.py:47
  464.8 0.0 all-gather.11.cloned.1.call-update
  464.8 0.5 all-gather.13.cloned.1.call-start
  465.3 39.3 %all-gather.11.cloned.1.call-done = f32[128,4096]{1,0:T(8,128)} async-done(((f32[128,512]{1,0:T(8,128)}), f32[128,4096]{1,0:T(8,128)}) %all-gather.11.cloned.1.call-update) | async-done | bytes 2097168 | tf_op jit(solution)/shard_map/all_gather | solution.py:48
  504.6 13.3 %multiply_reduce_fusion.4 = (f32[]{:T(128)}, f32[]{:T(128)}, f32[128,512]{1,0:T(8,128)S(1)}) fusion(f32[128,512]{1,0:T(8,128)} %get-tuple-element.14, f32[128,4096]{1,0:T(8,128)} %all-gather.11.cloned.1.call-done, f32[512,4096]{1,0:T(8,128)} %select_add_fusion), kind=kOutput, calls=%fused_computation.16 | convolution fusion | flops 3221487616 | bytes 11010056 | tf_op jit(solution)/shard_map/dot_general | solution.py:47
  518.0 74.2 %all-reduce.2 = (f32[]{:T(128)}, f32[]{:T(128)}) all-reduce(f32[]{:T(128)} %get-tuple-element.5, f32[]{:T(128)} %get-tuple-element.4), channel_id=1, replica_groups=mesh['tok'=16,'col'=8,'grp'=2] {'tok','col','grp'}, use_global_device_ids=true, to_apply=%region_4.5 | all-reduce | flops 2 | bytes 16 | tf_op jit(solution)/shard_map/psum | solution.py:61
  593.5 0.8 broadcast_multiply_fusion
  594.3 0.0 copy-start.7
  594.3 0.0 all-gather.13.cloned.1.call-update
  594.3 0.2 all-gather.15.cloned.1.call-start
  594.6 37.6 %all-gather.13.cloned.1.call-done = f32[128,4096]{1,0:T(8,128)} async-done(((f32[128,512]{1,0:T(8,128)}), f32[128,4096]{1,0:T(8,128)}) %all-gather.13.cloned.1.call-update) | async-done | bytes 2097168 | tf_op jit(solution)/shard_map/all_gather | solution.py:48
  632.2 13.4 %multiply_reduce_fusion.2 = (f32[]{:T(128)}, f32[]{:T(128)}, f32[128,512]{1,0:T(8,128)S(1)}) fusion(f32[128,512]{1,0:T(8,128)} %broadcast_multiply_fusion, f32[128,4096]{1,0:T(8,128)} %all-gather.13.cloned.1.call-done, f32[512,4096]{1,0:T(8,128)} %select_add_fusion), kind=kOutput, calls=%fused_computation.13 | convolution fusion | flops 3221487616 | bytes 11010056 | tf_op jit(solution)/shard_map/dot_general | solution.py:47
  645.6 74.2 %all-reduce.1 = (f32[]{:T(128)}, f32[]{:T(128)}) all-reduce(f32[]{:T(128)} %get-tuple-element.3, f32[]{:T(128)} %get-tuple-element.2), channel_id=1, replica_groups=mesh['tok'=16,'col'=8,'grp'=2] {'tok','col','grp'}, use_global_device_ids=true, to_apply=%region_8.9 | all-reduce | flops 2 | bytes 16 | tf_op jit(solution)/shard_map/psum | solution.py:61
  721.1 0.0 copy-start.1
  721.1 0.0 copy-start.3
  721.2 1.4 multiply_reduce_fusion.1
  722.6 0.0 copy-start.2
  722.6 0.0 all-gather.15.cloned.1.call-update
  722.6 0.0 all-gather.17.cloned.1.call-start
  722.6 0.0 copy-done.7
  722.7 0.7 gather_fusion
  723.4 0.7 broadcast_select_fusion
  724.1 0.0 all-gather.17.cloned.1.call-update
  724.1 0.3 reduce-scatter.5.cloned.1.call-start
  724.4 36.1 %all-gather.15.cloned.1.call-done = f32[128,4096]{1,0:T(8,128)} async-done(((f32[128,512]{1,0:T(8,128)}), f32[128,4096]{1,0:T(8,128)}) %all-gather.15.cloned.1.call-update) | async-done | bytes 2097168 | tf_op jit(solution)/shard_map/all_gather | solution.py:48
  760.5 13.3 %fusion = f32[]{:T(128)} fusion(f32[128,512]{1,0:T(8,128)} %get-tuple-element.13, f32[128,4096]{1,0:T(8,128)} %all-gather.15.cloned.1.call-done, f32[512,4096]{1,0:T(8,128)} %select_add_fusion), kind=kOutput, calls=%fused_computation.5 | convolution fusion | flops 3221356544 | bytes 10747908 | tf_op jit(solution)/shard_map/dot_general | solution.py:47
  773.8 74.2 %all-reduce = (f32[]{:T(128)}, f32[]{:T(128)}) all-reduce(f32[]{:T(128)} %get-tuple-element.12, f32[]{:T(128)} %fusion), channel_id=1, replica_groups=mesh['tok'=16,'col'=8,'grp'=2] {'tok','col','grp'}, use_global_device_ids=true, to_apply=%region_12.13 | all-reduce | flops 2 | bytes 16 | tf_op jit(solution)/shard_map/psum | solution.py:61
  849.3 0.0 copy-done.1
  849.3 0.0 copy-done.3
  849.3 0.0 copy-done.2
  849.3 0.1 fusion.3
  849.5 0.0 copy-start.5
  849.5 0.0 all-gather.17.cloned.1.call-done
  849.5 3.3 fusion.5
  852.8 0.0 reduce-scatter.5.cloned.1.call-update
  852.8 36.9 %reduce-scatter.5.cloned.1.call-done = f32[256,128]{1,0:T(8,128)} async-done(((f32[2048,128]{1,0:T(8,128)}), f32[256,128]{1,0:T(8,128)}) %reduce-scatter.5.cloned.1.call-update) | async-done | bytes 131088 | tf_op jit(solution)/shard_map/reduce_scatter | solution.py:71
  889.8 1.5 convert_element_type.15
  891.3 0.0 copy-done.5
  (5 shorter events, 0.0 us)
Async XLA Ops:
  7.2 298.2 %reduce-scatter.3.cloned.1.call-start = ((), (), s32[]{:S(2)}) async-start(), calls=%async_computation.4 | async-start | bytes 8650752 | tf_op jit(solution)/shard_map/reduce_scatter | solution.py:39
  9.0 149.5 %copy-start = (bf16[768,512]{1,0:T(8,128)(2,1)S(1)}, bf16[768,512]{1,0:T(8,128)(2,1)}, u32[]{:S(2)}) copy-start(bf16[768,512]{1,0:T(8,128)(2,1)} %param.4) | copy-start | bytes 2359300
  164.2 141.2 %copy-start.6 = (s32[1,4]{1,0:T(1,128)S(1)}, s32[1,4]{1,0:T(1,128)}, u32[]{:S(2)}) copy-start(s32[1,4]{1,0:T(1,128)} %param.6) | copy-start | bytes 52
  164.2 141.3 %copy-start.4 = (f32[128,512]{1,0:T(8,128)S(1)}, f32[128,512]{1,0:T(8,128)}, u32[]{:S(2)}) copy-start(f32[128,512]{1,0:T(8,128)} %param.5) | copy-start | bytes 786436
  164.2 244.0 %all-gather.9.cloned.1.call-start = ((), (), s32[]{:S(2)}) async-start(), calls=%async_computation.5 | async-start | bytes 8650752 | tf_op jit(solution)/shard_map/all_gather | solution.py:40
  305.3 146.0 %all-gather.7.cloned.1.call-start = ((), (), s32[]{:S(2)}) async-start(), calls=%async_computation.3 | async-start | bytes 2359296 | tf_op jit(solution)/shard_map/all_gather | solution.py:48
  306.3 198.4 %all-gather.11.cloned.1.call-start = ((), (), s32[]{:S(2)}) async-start(), calls=%async_computation.6 | async-start | bytes 2359296 | tf_op jit(solution)/shard_map/all_gather | solution.py:48
  464.8 167.4 %all-gather.13.cloned.1.call-start = ((), (), s32[]{:S(2)}) async-start(), calls=%async_computation.7 | async-start | bytes 2359296 | tf_op jit(solution)/shard_map/all_gather | solution.py:48
  594.3 128.3 %copy-start.7 = (s32[64]{0:T(128)S(1)}, s32[64]{0:T(128)}, u32[]{:S(2)}) copy-start(s32[64]{0:T(128)} %param.7) | copy-start | bytes 772
  594.3 166.1 %all-gather.15.cloned.1.call-start = ((), (), s32[]{:S(2)}) async-start(), calls=%async_computation.8 | async-start | bytes 2359296 | tf_op jit(solution)/shard_map/all_gather | solution.py:48
  721.1 128.2 %copy-start.1 = (f32[128,512]{1,0:T(8,128)S(1)}, f32[128,512]{1,0:T(8,128)}, u32[]{:S(2)}) copy-start(f32[128,512]{1,0:T(8,128)} %get-tuple-element.14) | copy-start | bytes 786436
  721.1 128.2 %copy-start.3 = (f32[128,512]{1,0:T(8,128)S(1)}, f32[128,512]{1,0:T(8,128)}, u32[]{:S(2)}) copy-start(f32[128,512]{1,0:T(8,128)} %broadcast_multiply_fusion) | copy-start | bytes 786436
  722.6 126.8 %copy-start.2 = (f32[128,512]{1,0:T(8,128)S(1)}, f32[128,512]{1,0:T(8,128)}, u32[]{:S(2)}) copy-start(f32[128,512]{1,0:T(8,128)} %get-tuple-element.13) | copy-start | bytes 786436
  722.6 126.9 %all-gather.17.cloned.1.call-start = ((), (), s32[]{:S(2)}) async-start(), calls=%async_computation.9 | async-start | bytes 2162688 | tf_op jit(solution)/shard_map/all_gather | solution.py:70
  724.1 165.6 %reduce-scatter.5.cloned.1.call-start = ((), (), s32[]{:S(2)}) async-start(), calls=%async_computation.10 | async-start | bytes 1179648 | tf_op jit(solution)/shard_map/reduce_scatter | solution.py:71
  849.5 41.8 %copy-start.5 = (bf16[128,512]{1,0:T(8,128)(2,1)}, bf16[128,512]{1,0:T(8,128)(2,1)S(1)}, u32[]{:S(2)}) copy-start(bf16[128,512]{1,0:T(8,128)(2,1)S(1)} %fusion.3) | copy-start | bytes 393220
Sparse Core Ops, SparseCore 0:
  164.3 140.9 reduce-scatter.2
  307.1 101.1 all-gather.8
  410.0 41.2 all-gather.6
  464.9 39.6 all-gather.10
  594.5 37.7 all-gather.12
  722.7 37.7 all-gather.14
  762.9 84.5 all-gather.16
  853.0 36.7 reduce-scatter.4
